TPU v7x, 32 devices: a whole 2x2x4 slice. The times are simulated.
32 devices in a mesh: batch: 4 (over y, x), ch: 8 (over z, core).
Axes of the slice: x: 2, y: 2, z: 4, core: 2. Of those that a mesh axis runs over, the one named last changes fastest.
Arguments:
- earlier: bfloat16 [4, 3840, 512], P('batch', 'ch'), may hold values from -6 to 6
- lengths: int32 [4], P('batch'), may hold values from 128 to 512, as said below
- lower_entry: bfloat16 [25, 768, 640], P(None, 'ch'), may hold values from -0.046875 to 0.046875
- lower_convs: bfloat16 [1, 25, 768, 768], P(None, None, 'ch'), may hold values from -0.046875 to 0.046875
- upper_convs: bfloat16 [2, 25, 768, 768], P(None, None, 'ch'), may hold values from -0.046875 to 0.046875
- lower_dense: bfloat16 [768, 3840], P('ch'), may hold values from -0.09375 to 0.09375
- upper_dense: bfloat16 [768, 4608], P('ch'), may hold values from -0.09375 to 0.09375
- lower_gain: float32 [11, 768], P(None, 'ch'), may hold values from 0.25 to 1.75
- lower_shift: float32 [11, 768], P(None, 'ch'), may hold values from -2 to 2
- upper_gain: float32 [12, 768], P(None, 'ch'), may hold values from 0.25 to 1.75
- upper_shift: float32 [12, 768], P(None, 'ch'), may hold values from -2 to 2
- cotangent: bfloat16 [4, 768, 512], P('batch', 'ch'), may hold values from -6 to 6
Outputs:
- final: bfloat16 [4, 768, 512], P('batch', 'ch')
- earlier_grad: float32 [4, 3840, 512], P('batch', 'ch')
- lower_entry_grad: float32 [25, 768, 640], P(None, 'ch', 'batch')
- lower_convs_grad: float32 [1, 25, 768, 768], P(None, None, 'ch', 'batch')
- upper_convs_grad: float32 [2, 25, 768, 768], P(None, None, 'ch', 'batch')
- lower_dense_grad: float32 [768, 3840], P('ch', 'batch')
- upper_dense_grad: float32 [768, 4608], P('ch', 'batch')
- lower_gain_grad: float32 [11, 768], P(None, 'ch')
- lower_shift_grad: float32 [11, 768], P(None, 'ch')
- upper_gain_grad: float32 [12, 768], P(None, 'ch')
- upper_shift_grad: float32 [12, 768], P(None, 'ch')
Inputs may be any that keep to these rules, and one draw needn't show every extreme that they name: `lengths`: one utterance has exactly 512 frames; the others have at least 128.
All inputs are finite; a program needn't handle non-finite values.
Results may differ from a plain program's by a relative error of at most 0.025.
Values may be sent and summed in bfloat16 or wider, within the bound.
A program may use at most 192 MiB of HBM per device.

v0:
```python
import jax
import jax.numpy as jnp
from jax import lax
from jax.sharding import PartitionSpec as P

epsilon = 0.001
unit_widths = (2, 2, 2, 3, 3, 4, 4, 5, 5)


def conv_apply(weight, inputs):
    kernel_taps = weight.shape[0]
    before = (kernel_taps - 1) // 2
    return lax.conv_general_dilated(
        inputs,
        weight,
        (1,),
        [(before, kernel_taps - 1 - before)],
        dimension_numbers=("NCH", "HOI", "NCH"),
        preferred_element_type=jnp.float32,
    )


def conv_back(weight, gradient):
    kernel_taps = weight.shape[0]
    before = (kernel_taps - 1) // 2
    return lax.conv_general_dilated(
        gradient,
        jnp.flip(weight, 0),
        (1,),
        [(kernel_taps - 1 - before, before)],
        dimension_numbers=("NCH", "HIO", "NCH"),
        preferred_element_type=jnp.float32,
    )


def conv_weight_grad(inputs, gradient, kernel_taps):
    before = (kernel_taps - 1) // 2
    padded = jnp.pad(inputs, ((0, 0), (0, 0), (before, kernel_taps - 1 - before)))
    return lax.conv_general_dilated(
        padded,
        gradient,
        (1,),
        [(0, 0)],
        dimension_numbers=("CNH", "IOH", "HCN"),
        preferred_element_type=jnp.float32,
    )


def spread(local_part):
    return lax.all_gather(local_part, "ch", axis=1, tiled=True)


def weight_gradient(inputs, grad_conv, kernel_taps):
    return lax.psum_scatter(
        conv_weight_grad(inputs, grad_conv, kernel_taps).astype(jnp.bfloat16),
        "batch",
        scatter_dimension=2,
        tiled=True,
    ).astype(jnp.float32)


def carry_back(weight, grad_conv, additional):
    partial_sum = conv_back(weight, grad_conv)
    if additional is not None:
        partial_sum = partial_sum + additional
    return lax.psum_scatter(
        partial_sum.astype(jnp.bfloat16), "ch", scatter_dimension=1, tiled=True
    ).astype(jnp.float32)


def block_forward(
    entry_input,
    conv_list,
    dense_weight,
    source_pieces,
    gain_rows,
    shift_rows,
    validity,
    local_count,
):
    subs = len(conv_list)
    branch_terms = []
    offset = 0
    for source_piece in source_pieces:
        channels = source_piece.shape[1]
        branch_terms.append(
            jnp.einsum(
                "oi,uit->uot",
                dense_weight[:, offset : offset + channels],
                source_piece,
                preferred_element_type=jnp.float32,
            )
        )
        offset = offset + channels
    branch_terms = jnp.stack(branch_terms)
    dense_first = jnp.sum(branch_terms * validity, axis=(1, 3))
    dense_second = jnp.sum(branch_terms * branch_terms * validity, axis=(1, 3))
    inputs = []
    normed = []
    scales = []
    activity = []
    gathered = entry_input
    for sub_index in range(subs):
        if sub_index > 0:
            gathered = spread((jax.nn.silu(activity[-1]) * validity).astype(jnp.bfloat16))
        outputs = conv_apply(conv_list[sub_index], gathered)
        first_sum = jnp.sum(outputs * validity, axis=(0, 2))
        second = jnp.sum(outputs * outputs * validity, axis=(0, 2))
        if sub_index == 0:
            first_sum, second, dense_first, dense_second, frame_count = lax.psum(
                (first_sum, second, dense_first, dense_second, local_count), "batch"
            )
            dense_average = dense_first / frame_count
            dense_scaling = lax.rsqrt(
                dense_second / frame_count - dense_average * dense_average + epsilon
            )
            dense_centred = (branch_terms - dense_average[:, None, :, None]) * dense_scaling[
                :, None, :, None
            ]
        else:
            first_sum, second = lax.psum((first_sum, second), "batch")
        average = first_sum / frame_count
        scaling = lax.rsqrt(second / frame_count - average * average + epsilon)
        centred = (outputs - average[:, None]) * scaling[:, None]
        inputs.append(gathered)
        normed.append(centred)
        scales.append(scaling)
        activity.append(centred * gain_rows[sub_index][:, None] + shift_rows[sub_index][:, None])
    residual = jnp.sum(
        dense_centred * gain_rows[subs:][:, None, :, None] + shift_rows[subs:][:, None, :, None],
        axis=0,
    )
    pre_sum = activity[-1] + residual
    result = jax.nn.silu(pre_sum) * validity
    return (
        result,
        (inputs, normed, scales, activity, dense_centred, dense_scaling, pre_sum),
        frame_count,
    )


def block_backward(
    grad_out, conv_list, dense_weight, source_pieces, gain_rows, validity, frame_count, kept_state
):
    inputs, normed, scales, activity, dense_centred, dense_scaling, pre_sum = kept_state
    subs = len(conv_list)
    squash = jax.nn.sigmoid(pre_sum)
    grad_sum = grad_out * validity * squash * (1.0 + pre_sum * (1.0 - squash))
    shift_total, gain_total, gain_dense = lax.psum(
        (
            jnp.sum(grad_sum, axis=(0, 2)),
            jnp.sum(grad_sum * normed[-1], axis=(0, 2)),
            jnp.sum(grad_sum[None] * dense_centred, axis=(1, 3)),
        ),
        "batch",
    )
    factor = (dense_scaling * gain_rows[subs:])[:, None, :, None]
    grad_terms = (
        factor
        * (
            grad_sum[None]
            - validity[None]
            * (shift_total[:, None] + dense_centred * gain_dense[:, None, :, None])
            / frame_count
        )
    ).astype(jnp.bfloat16)
    dense_parts = []
    source_parts = []
    offset = 0
    for source_index, source_piece in enumerate(source_pieces):
        channels = source_piece.shape[1]
        dense_parts.append(
            jnp.einsum(
                "uot,uit->oi",
                grad_terms[source_index],
                source_piece,
                preferred_element_type=jnp.float32,
            )
        )
        source_parts.append(
            jnp.einsum(
                "oi,uot->uit",
                dense_weight[:, offset : offset + channels],
                grad_terms[source_index],
                preferred_element_type=jnp.float32,
            )
        )
        offset = offset + channels
    dense_grad = lax.psum_scatter(
        jnp.concatenate(dense_parts, axis=1).astype(jnp.bfloat16),
        "batch",
        scatter_dimension=1,
        tiled=True,
    ).astype(jnp.float32)
    weight_grads = [None] * subs
    gain_sums = [None] * subs
    shift_sums = [None] * subs
    grad_pre = grad_sum
    grad_inner = grad_sum
    shift_now = shift_total
    gain_now = gain_total
    grad_conv = None
    for sub_index in reversed(range(subs)):
        if sub_index < subs - 1:
            squash = jax.nn.sigmoid(activity[sub_index])
            grad_pre = grad_inner * validity * squash * (1.0 + activity[sub_index] * (1.0 - squash))
            shift_now, gain_now = lax.psum(
                (
                    jnp.sum(grad_pre, axis=(0, 2)),
                    jnp.sum(grad_pre * normed[sub_index], axis=(0, 2)),
                ),
                "batch",
            )
        shift_sums[sub_index] = shift_now
        gain_sums[sub_index] = gain_now
        grad_conv = (
            (scales[sub_index] * gain_rows[sub_index])[:, None]
            * (
                grad_pre
                - validity
                * (shift_now[:, None] + normed[sub_index] * gain_now[:, None])
                / frame_count
            )
        ).astype(jnp.bfloat16)
        weight_grads[sub_index] = weight_gradient(
            inputs[sub_index], grad_conv, conv_list[sub_index].shape[0]
        )
        if sub_index > 0:
            grad_inner = carry_back(conv_list[sub_index], grad_conv, None)
    gain_grad = jnp.concatenate([jnp.stack(gain_sums), gain_dense], axis=0)
    shift_grad = jnp.concatenate(
        [jnp.stack(shift_sums), jnp.broadcast_to(shift_total, gain_dense.shape)], axis=0
    )
    return (weight_grads, dense_grad, gain_grad, shift_grad, grad_conv, source_parts)


def per_device(
    earlier,
    lengths,
    lower_entry,
    lower_convs,
    upper_convs,
    lower_dense,
    upper_dense,
    lower_gain,
    lower_shift,
    upper_gain,
    upper_shift,
    cotangent,
):
    frames = earlier.shape[2]
    validity = (
        lax.broadcasted_iota(jnp.int32, (earlier.shape[0], frames), 1) < lengths[:, None]
    ).astype(jnp.float32)[:, None, :]
    local_count = jnp.sum(lengths).astype(jnp.float32)
    masked = (earlier.astype(jnp.float32) * validity).astype(jnp.bfloat16)
    sources_full = lax.all_gather(masked, "ch", axis=1, tiled=True)
    unit_channels = sources_full.shape[1] // 30
    source_pieces = []
    offset = 0
    for factor in unit_widths:
        source_pieces.append(sources_full[:, offset : offset + factor * unit_channels])
        offset = offset + factor * unit_channels
    lower_list = [lower_entry] + [lower_convs[0]]
    upper_list = [upper_convs[sub_index] for sub_index in range(upper_convs.shape[0])]
    lower_out, lower_kept, frame_count = block_forward(
        source_pieces[-1],
        lower_list,
        lower_dense,
        source_pieces,
        lower_gain,
        lower_shift,
        validity,
        local_count,
    )
    middle_full = spread(lower_out.astype(jnp.bfloat16))
    upper_pieces = source_pieces + [middle_full]
    upper_out, upper_kept, frame_count = block_forward(
        middle_full,
        upper_list,
        upper_dense,
        upper_pieces,
        upper_gain,
        upper_shift,
        validity,
        local_count,
    )
    upper_weights, upper_dense_grad, upper_gain_grad, upper_shift_grad, upper_head, upper_parts = (
        block_backward(
            cotangent.astype(jnp.float32),
            upper_list,
            upper_dense,
            upper_pieces,
            upper_gain,
            validity,
            frame_count,
            upper_kept,
        )
    )
    middle_grad = carry_back(upper_list[0], upper_head, upper_parts[-1])
    lower_weights, lower_dense_grad, lower_gain_grad, lower_shift_grad, lower_head, lower_parts = (
        block_backward(
            middle_grad,
            lower_list,
            lower_dense,
            source_pieces,
            lower_gain,
            validity,
            frame_count,
            lower_kept,
        )
    )
    entry_part = conv_back(lower_entry, lower_head)
    combined = [
        lower_parts[source_index] + upper_parts[source_index]
        for source_index in range(len(source_pieces))
    ]
    combined[-1] = combined[-1] + entry_part
    source_grad = (
        lax.psum_scatter(
            jnp.concatenate(combined, axis=1).astype(jnp.bfloat16),
            "ch",
            scatter_dimension=1,
            tiled=True,
        ).astype(jnp.float32)
        * validity
    )
    return (
        upper_out.astype(jnp.bfloat16),
        source_grad,
        lower_weights[0],
        jnp.stack(lower_weights[1:]),
        jnp.stack(upper_weights),
        lower_dense_grad,
        upper_dense_grad,
        lower_gain_grad,
        lower_shift_grad,
        upper_gain_grad,
        upper_shift_grad,
    )


def solution(mesh):
    placed = (
        P("batch", "ch", None),
        P("batch"),
        P(None, "ch", None),
        P(None, None, "ch", None),
        P(None, None, "ch", None),
        P("ch", None),
        P("ch", None),
        P(None, "ch"),
        P(None, "ch"),
        P(None, "ch"),
        P(None, "ch"),
        P("batch", "ch", None),
    )
    return jax.shard_map(
        per_device,
        mesh=mesh,
        in_specs=placed,
        out_specs=(
            P("batch", "ch", None),
            P("batch", "ch", None),
            P(None, "ch", "batch"),
            P(None, None, "ch", "batch"),
            P(None, None, "ch", "batch"),
            P("ch", "batch"),
            P("ch", "batch"),
            P(None, "ch"),
            P(None, "ch"),
            P(None, "ch"),
            P(None, "ch"),
        ),
        check_vma=False,
    )
```

profile of v0, /device:TPU:25, one launch (start us, length us, event | category | flops | bytes accessed | tf_op | source)
XLA Modules:
  0.0 902.2 jit_solution(4205240511739255536)
XLA Ops:
  13.5 40.9 %all-gather.2.cloned.1.call-done = bf16[1,3840,512]{2,1,0:T(8,128)(2,1)} async-done(((bf16[1,480,512]{2,1,0:T(8,128)(2,1)}), bf16[1,3840,512]{2,1,0:T(8,128)(2,1)}) %all-gather.2.cloned.1.call-update) | async-done | bytes 3932176 | tf_op jit(solution)/shard_map/all_gather | solution.py:257
  57.9 3.2 reshape.1918
  65.2 6.5 fusion.297
  76.9 8.2 all-reduce.7
  93.8 18.0 %all_gather.13 = bf16[1,768,512]{2,1,0:T(8,128)(2,1)S(1)} all-gather(bf16[1,96,512]{2,1,0:T(8,128)(2,1)S(1)} %fusion.218), channel_id=1, replica_groups=mesh['batch'=4,'ch'=8] {'ch'}, dimensions={1}, use_global_device_ids=true | all-gather | bytes 884736 | tf_op jit(solution)/shard_map/all_gather | solution.py:50
  114.2 3.8 reshape.1919
  118.0 3.1 copy.227
  122.2 8.6 fusion.298
  151.3 10.6 %all-reduce.6 = (f32[9,96]{1,0:T(8,128)S(1)}, f32[9,96]{1,0:T(8,128)S(1)}, f32[96]{0:T(128)S(1)}, f32[96]{0:T(128)S(1)}) all-reduce(f32[9,96]{1,0:T(8,128)S(1)} %get-tuple-element.58, f32[9,96]{1,0:T(8,128)S(1)} %get-tuple-element.57, f32[96]{0:T(128)S(1)} %get-tuple-element.72, ...), channel_id=1, replica_groups=mesh['batch'=4,'ch'=8] {'batch'}, use_global_device_ids=true, to_apply=%region_10.11 | all-reduce | flops 1920 | bytes 15360 | tf_op jit(solution)/shard_map/psum | solution.py:110
  174.0 19.8 %all_gather.14 = bf16[1,768,512]{2,1,0:T(8,128)(2,1)S(1)} all-gather(bf16[1,96,512]{2,1,0:T(8,128)(2,1)S(1)} %multiply_convert_fusion.4), channel_id=1, replica_groups=mesh['batch'=4,'ch'=8] {'ch'}, dimensions={1}, use_global_device_ids=true | all-gather | bytes 884736 | tf_op jit(solution)/shard_map/all_gather | solution.py:50
  196.2 3.8 reshape.1920
  200.1 3.1 copy.237
  204.2 8.6 fusion.299
  221.4 7.0 all-reduce.5
  237.7 17.9 %all_gather.15 = bf16[1,768,512]{2,1,0:T(8,128)(2,1)S(1)} all-gather(bf16[1,96,512]{2,1,0:T(8,128)(2,1)S(1)} %fusion.219), channel_id=1, replica_groups=mesh['batch'=4,'ch'=8] {'ch'}, dimensions={1}, use_global_device_ids=true | all-gather | bytes 884736 | tf_op jit(solution)/shard_map/all_gather | solution.py:50
  257.9 3.8 reshape.1921
  261.8 3.1 copy.246
  265.9 8.6 fusion.300
  295.5 11.0 %all-reduce.4 = (f32[10,96]{1,0:T(8,128)S(1)}, f32[10,96]{1,0:T(8,128)S(1)}, f32[96]{0:T(128)S(1)}, f32[96]{0:T(128)S(1)}) all-reduce(f32[10,96]{1,0:T(8,128)S(1)} %get-tuple-element.56, f32[10,96]{1,0:T(8,128)S(1)} %get-tuple-element.55, f32[96]{0:T(128)S(1)} %get-tuple-element.68, ...), channel_id=1, replica_groups=mesh['batch'=4,'ch'=8] {'batch'}, use_global_device_ids=true, to_apply=%region_23.24 | all-reduce | flops 2112 | bytes 16896 | tf_op jit(solution)/shard_map/psum | solution.py:110
  323.4 8.3 all-reduce.3
  344.7 4.4 select_convert_fusion.1
  354.5 4.8 copy.337
  375.7 19.5 %reduce-scatter.31.cloned.1.call-done = bf16[96,512]{1,0:T(8,128)(2,1)} async-done(((bf16[768,512]{1,0:T(8,128)(2,1)}), bf16[96,512]{1,0:T(8,128)(2,1)}) %reduce-scatter.31.cloned.1.call-update) | async-done | bytes 98320
  398.7 9.1 %all-reduce.2 = (f32[96]{0:T(128)}, f32[96]{0:T(128)}, f32[10,96]{1,0:T(8,128)}) all-reduce(f32[96]{0:T(128)} %get-tuple-element.64, f32[96]{0:T(128)} %get-tuple-element.63, f32[10,96]{1,0:T(8,128)} %multiply_reduce_fusion), channel_id=1, replica_groups=mesh['batch'=4,'ch'=8] {'batch'}, use_global_device_ids=true, to_apply=%region_33.34 | all-reduce | flops 1152 | bytes 9216 | tf_op jit(solution)/shard_map/psum | solution.py:207
  420.9 4.4 fusion.24
  435.8 4.8 copy.339
  446.3 4.8 copy.309
  468.9 4.1 reduce-scatter.33.cloned.1.call-done
  475.8 8.8 all-reduce.1
  493.6 4.4 select_convert_fusion
  503.5 4.8 copy.341
  530.1 10.4 %reduce-scatter.35.cloned.1.call-done = bf16[96,512]{1,0:T(8,128)(2,1)} async-done(((bf16[768,512]{1,0:T(8,128)(2,1)}), bf16[96,512]{1,0:T(8,128)(2,1)}) %reduce-scatter.35.cloned.1.call-update) | async-done | bytes 98320
  543.9 9.1 %all-reduce = (f32[9,96]{1,0:T(8,128)S(1)}, f32[96]{0:T(128)}, f32[96]{0:T(128)}) all-reduce(f32[9,96]{1,0:T(8,128)} %multiply_reduce_fusion.3, f32[96]{0:T(128)} %get-tuple-element.60, f32[96]{0:T(128)} %get-tuple-element.59), channel_id=1, replica_groups=mesh['batch'=4,'ch'=8] {'batch'}, use_global_device_ids=true, to_apply=%region_42.43 | all-reduce | flops 1056 | bytes 8448 | tf_op jit(solution)/shard_map/psum | solution.py:149
  569.7 21.6 %convolution_convert_fusion = bf16[25,96,768]{1,2,0:T(8,128)(2,1)} fusion(bf16[1,768,512]{1,0,2:T(2,128)(2,1)} %copy.309, bf16[1,96,512]{1,0,2:T(2,128)(2,1)S(1)} %copy-done.40), kind=kOutput, calls=%fused_computation.17 | convolution fusion | flops 1866276864 | bytes 4571136 | tf_op jit(solution)/shard_map/conv_general_dilated | solution.py:39
  591.3 4.8 copy.307
  596.1 4.8 copy.305
  600.8 3.7 copy.397
  605.6 21.6 %convolution_convert_fusion.1 = bf16[25,96,768]{1,2,0:T(8,128)(2,1)} fusion(bf16[1,768,512]{1,0,2:T(2,128)(2,1)} %copy.307, bf16[1,96,512]{1,0,2:T(2,128)(2,1)S(1)} %copy.308), kind=kOutput, calls=%fused_computation.18 | convolution fusion | flops 1866276864 | bytes 4571136 | tf_op jit(solution)/shard_map/conv_general_dilated | solution.py:39
  628.3 21.6 %convolution_convert_fusion.2 = bf16[25,96,768]{1,2,0:T(8,128)(2,1)} fusion(bf16[1,768,512]{1,0,2:T(2,128)(2,1)} %copy.305, bf16[1,96,512]{1,0,2:T(2,128)(2,1)S(1)} %copy.306), kind=kOutput, calls=%fused_computation.19 | convolution fusion | flops 1866276864 | bytes 4571136 | tf_op jit(solution)/shard_map/conv_general_dilated | solution.py:39
  655.6 19.8 %convolution_convert_fusion.3 = bf16[25,96,640]{1,2,0:T(8,128)(2,1)} fusion(bf16[1,640,512]{1,0,2:T(2,128)(2,1)} %copy.397, bf16[1,96,512]{1,0,2:T(2,128)(2,1)S(1)} %copy.304), kind=kOutput, calls=%fused_computation.20 | convolution fusion | flops 1555230720 | bytes 3825664 | tf_op jit(solution)/shard_map/conv_general_dilated | solution.py:39
  735.1 17.0 %copy.343 = bf16[1,3840,512]{2,0,1:T(2,128)(2,1)} copy(bf16[1,3840,512]{1,2,0:T(8,128)(2,1)} %fusion.38) | data formatting | bytes 7864320
  752.2 6.6 copy.409
  765.8 4.6 maximum_convert_fusion
  770.4 6.3 copy.312
  776.7 13.2 %reduce-scatter.25.cloned.1.call-done = bf16[25,96,192]{1,2,0:T(8,128)(2,1)} async-done(((bf16[25,96,768]{1,2,0:T(8,128)(2,1)}), bf16[25,96,192]{1,2,0:T(8,128)(2,1)}) %reduce-scatter.25.cloned.1.call-update) | async-done | bytes 921616 | tf_op jit(solution)/shard_map/reduce_scatter | solution.py:54
  792.9 3.3 copy.311
  796.2 48.8 %reduce-scatter.23.cloned.1.call-done = bf16[25,96,160]{1,2,0:T(8,128)(2,1)} async-done(((bf16[25,96,640]{1,2,0:T(8,128)(2,1)}), bf16[25,96,160]{1,2,0:T(8,128)(2,1)}) %reduce-scatter.23.cloned.1.call-update) | async-done | bytes 768016 | tf_op jit(solution)/shard_map/reduce_scatter | solution.py:54
  847.7 44.9 %reduce-scatter.37.cloned.1.call-done = bf16[480,512]{1,0:T(8,128)(2,1)} async-done(((bf16[3840,512]{1,0:T(8,128)(2,1)}), bf16[480,512]{1,0:T(8,128)(2,1)}) %reduce-scatter.37.cloned.1.call-update) | async-done | bytes 491536
  (391 shorter events, 352.4 us)
Async XLA Ops:
  7.2 58.0 %copy-start = (bf16[25,96,640]{2,1,0:T(8,128)(2,1)S(1)}, bf16[25,96,640]{2,1,0:T(8,128)(2,1)}, u32[]{:S(2)}) copy-start(bf16[25,96,640]{2,1,0:T(8,128)(2,1)} %param.14) | copy-start | bytes 9216004
  7.2 47.3 %all-gather.2.cloned.1.call-start = ((), (), s32[]{:S(2)}) async-start(), calls=%async_computation.10 | async-start | bytes 4423680 | tf_op jit(solution)/shard_map/all_gather | solution.py:257
  8.0 545.0 %copy-start.23 = (f32[512]{0:T(512)}, f32[512]{0:T(512)S(1)}, u32[]{:S(2)}) copy-start(f32[512]{0:T(512)S(1)} %fusion.261) | copy-start | bytes 6148
  10.0 385.1 %reduce-scatter.31.cloned.1.call-start = ((), (), s32[]{:S(2)}) async-start(), calls=%async_computation.15 | async-start | bytes 884736
  57.9 7.3 copy-start.64
  71.7 13.4 %copy-start.49 = (f32[11,96]{1,0:T(8,128)S(1)}, f32[11,96]{1,0:T(8,128)}, u32[]{:S(2)}) copy-start(f32[11,96]{1,0:T(8,128)} %param.19) | copy-start | bytes 12676
  88.2 355.4 %copy-start.11 = (f32[8,67,96]{2,0,1:T(8,128)}, f32[8,67,96]{2,0,1:T(8,128)S(1)}, u32[]{:S(2)}) copy-start(f32[8,67,96]{2,0,1:T(8,128)S(1)} %get-tuple-element.109) | copy-start | bytes 617476
  138.2 4.8 copy-start.20
  146.8 4.4 copy-start.34
  146.8 4.4 copy-start.36
  168.6 5.4 copy-start.22
  200.1 4.2 copy-start.65
  212.8 15.6 %copy-start.50 = (f32[12,96]{1,0:T(8,128)S(1)}, f32[12,96]{1,0:T(8,128)}, u32[]{:S(2)}) copy-start(f32[12,96]{1,0:T(8,128)} %param.21) | copy-start | bytes 13828
  281.9 4.8 copy-start.16
  288.0 5.4 copy-start.4
  293.3 16.5 %copy-start.54 = (f32[96]{0:T(128)S(1)}, f32[96]{0:T(128)}, u32[]{:S(2)}) copy-start(f32[96]{0:T(128)} %get-tuple-element.154) | copy-start | bytes 1156
  307.8 11.3 %copy-start.41 = (f32[10,96]{1,0:T(8,128)}, f32[10,96]{1,0:T(8,128)S(1)}, u32[]{:S(2)}) copy-start(f32[10,96]{1,0:T(8,128)S(1)} %get-tuple-element.111) | copy-start | bytes 11524
  308.5 10.6 %copy-start.44 = (f32[10,96]{1,0:T(8,128)}, f32[10,96]{1,0:T(8,128)S(1)}, u32[]{:S(2)}) copy-start(f32[10,96]{1,0:T(8,128)S(1)} %add_rsqrt_fusion) | copy-start | bytes 11524
  361.8 111.2 %reduce-scatter.33.cloned.1.call-start = ((), (), s32[]{:S(2)}) async-start(), calls=%async_computation.16 | async-start | bytes 884736
  429.9 3.8 copy-start.9
  443.1 97.4 %reduce-scatter.35.cloned.1.call-start = ((), (), s32[]{:S(2)}) async-start(), calls=%async_computation.17 | async-start | bytes 884736
  444.5 6.6 copy-start.17
  486.0 7.6 copy-start.66
  491.4 6.6 copy-start.28
  510.7 250.0 %reduce-scatter.41.cloned.1.call-start = ((), (), s32[]{:S(2)}) async-start(), calls=%async_computation.20 | async-start | bytes 1474560
  514.7 8.4 copy-start.5
  523.1 4.4 copy-start.43
  527.4 14.1 %copy-start.37 = (f32[1,536,96]{1,2,0:T(8,128)S(1)}, f32[1,536,96]{1,2,0:T(8,128)}, u32[]{:S(2)}) copy-start(f32[1,536,96]{1,2,0:T(8,128)} %reshape.1903) | copy-start | bytes 617476
  527.4 25.6 %copy-start.45 = (f32[9,96]{1,0:T(8,128)S(1)}, f32[9,96]{1,0:T(8,128)}, u32[]{:S(2)}) copy-start(f32[9,96]{1,0:T(8,128)} %get-tuple-element.101) | copy-start | bytes 10372
  527.4 25.6 %copy-start.52 = (f32[96]{0:T(128)S(1)}, f32[96]{0:T(128)}, u32[]{:S(2)}) copy-start(f32[96]{0:T(128)} %get-tuple-element.78) | copy-start | bytes 1156
  527.4 236.5 %reduce-scatter.39.cloned.1.call-start = ((), (), s32[]{:S(2)}) async-start(), calls=%async_computation.19 | async-start | bytes 1228800
  553.0 8.6 copy-start.47
  553.0 8.5 copy-start.6
  556.0 10.3 %copy-start.15 = (bf16[9,1,96,512]{3,2,1,0:T(8,128)(2,1)}, bf16[9,1,96,512]{3,2,1,0:T(8,128)(2,1)S(1)}, u32[]{:S(2)}) copy-start(bf16[9,1,96,512]{3,2,1,0:T(8,128)(2,1)S(1)} %multiply_convert_fusion.1) | copy-start | bytes 2654212
  569.5 196.3 %reduce-scatter.29.cloned.1.call-start = ((), (), s32[]{:S(2)}) async-start(), calls=%async_computation.14 | async-start | bytes 6144000 | tf_op jit(solution)/shard_map/reduce_scatter | solution.py:54
  604.6 161.3 %reduce-scatter.27.cloned.1.call-start = ((), (), s32[]{:S(2)}) async-start(), calls=%async_computation.13 | async-start | bytes 6144000 | tf_op jit(solution)/shard_map/reduce_scatter | solution.py:54
  627.2 162.6 %reduce-scatter.25.cloned.1.call-start = ((), (), s32[]{:S(2)}) async-start(), calls=%async_computation.12 | async-start | bytes 6144000 | tf_op jit(solution)/shard_map/reduce_scatter | solution.py:54
  649.9 195.1 %reduce-scatter.23.cloned.1.call-start = ((), (), s32[]{:S(2)}) async-start(), calls=%async_computation.11 | async-start | bytes 5120000 | tf_op jit(solution)/shard_map/reduce_scatter | solution.py:54
  655.5 20.0 %copy-start.31 = (bf16[1,96,512]{2,1,0:T(8,128)(2,1)}, bf16[1,96,512]{2,1,0:T(8,128)(2,1)S(1)}, u32[]{:S(2)}) copy-start(bf16[1,96,512]{2,1,0:T(8,128)(2,1)S(1)} %fusion.181) | copy-start | bytes 294916
  675.5 217.2 %reduce-scatter.37.cloned.1.call-start = ((), (), s32[]{:S(2)}) async-start(), calls=%async_computation.18 | async-start | bytes 4423680
  718.4 7.9 copy-start.19
  718.4 8.7 copy-start.18
  758.9 3.9 copy-start.48
  758.9 3.8 copy-start.59
  758.9 3.8 copy-start.63
  758.9 4.4 copy-start.53
  758.9 4.4 copy-start.61
  796.2 98.0 %copy-start.25 = (f32[512]{0:T(512)S(1)}, f32[512]{0:T(512)}, u32[]{:S(2)}) copy-start(f32[512]{0:T(512)} %copy-done.23) | copy-start | bytes 6148
  (31 other events, 46.9 us)
Sparse Core Ops, SparseCore 0:
  10.2 44.1 all-gather.1
  361.9 33.2 reduce-scatter.30
  443.2 29.6 reduce-scatter.32
  510.9 29.5 reduce-scatter.34
  543.5 29.2 reduce-scatter.40
  575.9 27.2 reduce-scatter.38
  607.1 58.6 reduce-scatter.28
  669.1 58.6 reduce-scatter.26
  731.1 58.6 reduce-scatter.24
  793.1 51.8 reduce-scatter.22
  847.4 45.2 reduce-scatter.36
where the time goes:
time: 919 us; the launch traced here: 902 us
  local copies, waits for them, and re-layouts  279 us (30%)
  matrix products  218 us (24%)
  waiting for transfers between devices  182 us (20%)
  blocking collectives  128 us (14%)
  other arithmetic  77.5 us (8%)
  between operations  16.1 us (2%)
    unnamed x162, local copies, waits for them, and re-layouts  92.6 us
    conv_general_dilated x4, matrix products, conv_weight_grad(): lax.conv_general_dilated(padded, gradient, (1,), [(0, 0)], dimension_numb...  84.6 us
    unnamed x17, waiting for transfers between devices  79 us
    reduce_scatter x4, waiting for transfers between devices, weight_gradient(): lax.psum_scatter(conv_weight_grad(inputs, grad_conv, kernel_taps).astype(...  61.9 us
    all_gather x3, blocking collectives, spread(): return lax.all_gather(local_part, 'ch', axis=1, tiled=True)  55.8 us
    conv_general_dilated x20, local copies, waits for them, and re-layouts, conv_apply(): lax.conv_general_dilated(inputs, weight, (1,), [(before, kernel_taps - 1...  44.4 us
    all_gather x1, waiting for transfers between devices, per_device(): sources_full = lax.all_gather(masked, 'ch', axis=1, tiled=True)  40.9 us
    psum x4, blocking collectives, block_forward(): lax.psum((first_sum, second, dense_first, dense_second, local_count), 'ba...  36.8 us
  transfers between devices with their start and end apart: 11, of which 7 were waited for; matrix products, arithmetic and copies ran while one was open for 32% of the time, Pallas kernels for 0%

commit v1 on v0

v1 whole, which is shorter than its diff:
```python
import functools
import math

import jax
import jax.numpy as jnp
from jax import lax
from jax.experimental import pallas as pl
from jax.experimental.pallas import tpu as pltpu
from jax.sharding import PartitionSpec as P

EPS = 0.001
WIDTHS = (2, 2, 2, 3, 3, 4, 4, 5, 5)
MESH = pl.DeviceIdType.MESH
F32 = jnp.float32
BF16 = jnp.bfloat16
RB = 16
LANES = 128


def shifted(x, by):
    if by == 0:
        return x
    frames = x.shape[1]
    lane = lax.broadcasted_iota(jnp.int32, x.shape, 1)
    rolled = pltpu.roll(x, (-by) % frames, 1)
    keep = (lane < frames - by) if by > 0 else (lane >= -by)
    return jnp.where(keep, rolled, jnp.zeros_like(rolled))


def squash(v):
    return 0.5 * jnp.tanh(0.5 * v) + 0.5


def dot(a, b):
    return jnp.dot(a, b, preferred_element_type=F32)


def dot_first(a, b):
    return lax.dot_general(a, b, (((0,), (0,)), ((), ())), preferred_element_type=F32)


def dot_last(a, b):
    return lax.dot_general(a, b, (((1,), (1,)), ((), ())), preferred_element_type=F32)


class Plan:
    def __init__(self, nb, nc, own, frames, taps, cw, pre):
        self.nb, self.nc, self.nz = nb, nc, nc // 2
        self.own, self.frames, self.taps, self.cw, self.pre = own, frames, taps, cw, pre
        self.wide = cw * nc
        self.all = own * nc
        unit = self.all // 30
        self.pieces = []
        at = 0
        for w in WIDTHS:
            self.pieces.append((at, w * unit))
            at += w * unit
        self.head = self.all - pre
        self.full = self.head // own
        self.part = self.head % own
        step = math.gcd(own, self.head)
        self.step = step // 2 if step % 32 == 0 else step
        self.late = []
        for row in range(self.head, self.all, self.step):
            c = row // own
            self.late.append((c // 2, c % 2, row))
        self.iw0 = pre // nb
        self.iw = self.wide // nb
        self.group = 5
        self.sems = 0
        nz = self.nz
        self.s_entry = self.take(2 * len(self.late))
        self.s_rest = self.take(2 * nz)
        self.s_x = [self.take(2 * nz) for _ in range(3)]
        self.s_sum = [self.take(nb) for _ in range(8)]
        self.s_xs = [self.take(nb) for _ in range(4)]
        self.s_dy = [self.take(nb) for _ in range(4)]
        self.s_rs = [self.take(2 * nz) for _ in range(3)]
        self.s_dp = self.take(2 * nz)
        self.s_tail = self.take(3 * len(self.late))
        self.s_dr = [self.take(nb) for _ in range(2)]

    def take(self, count):
        base = self.sems
        self.sems += count
        return base


def up16(n):
    return (n + 15) // 16 * 16


SUM_ROWS = (8, 40, 8, 8, 16, 8, 16, 8)


def kernel(
    pn,
    length_ref,
    earlier_hbm,
    w0_hbm,
    w1_hbm,
    w23_hbm,
    rl_hbm,
    ru_hbm,
    lg_ref,
    lsh_ref,
    ug_ref,
    ush_ref,
    cot_ref,
    final_ref,
    egrad_hbm,
    g0_hbm,
    g1_hbm,
    g23_hbm,
    rlg_ref,
    rug_ref,
    lgg_ref,
    lsg_ref,
    ugg_ref,
    usg_ref,
    w0,
    w1,
    w2,
    w3,
    rcat,
    src,
    x1,
    x2,
    x3,
    big,
    resid,
    rmid,
    ys,
    dbuf,
    dgrp,
    drcat,
    dpart,
    dpsib,
    dprecv,
    dxpart,
    dxsib,
    dxrecv,
    tailsib,
    tailrecv,
    dyg,
    xs0,
    xs,
    xst,
    drs,
    drr,
    sums,
    colbuf,
    rowbuf,
    kcol,
    prm,
    hold,
    gout,
    gst,
    lsem,
    osem,
    ss,
    rs,
):
    nb, nc, nz = pn.nb, pn.nc, pn.nz
    T, K, C, E = pn.frames, pn.taps, pn.cw, pn.own
    WIDE, PRE, HEAD = pn.wide, pn.pre, pn.head
    b = lax.axis_index("batch")
    c = lax.axis_index("ch")
    z = c // 2
    q = lax.rem(c, 2)
    sib = z * 2 + 1 - q
    other = 1 - q

    def mult(v, m=16):
        return pl.multiple_of(v, m)

    def rcopy(source, target, i_send, i_recv, device):
        return pltpu.make_async_remote_copy(
            src_ref=source,
            dst_ref=target,
            send_sem=ss.at[i_send],
            recv_sem=rs.at[i_recv],
            device_id=device,
            device_id_type=MESH,
        )

    def chip(zz, qq):
        return {"ch": zz * 2 + qq}

    local_loads = []

    def load(source, target):
        cp = pltpu.make_async_copy(source, target, lsem.at[len(local_loads)])
        local_loads.append(cp)
        cp.start()
        return cp

    raw = dpart
    ld_raw = load(earlier_hbm, raw.at[0:E])
    ld_w0 = load(w0_hbm, w0.at[0 : K * C])
    ld_w0l = load(rl_hbm.at[:, HEAD : HEAD + PRE], w0.at[K * C : (K + 1) * C])
    ld_w0u = load(ru_hbm.at[:, HEAD : HEAD + PRE], w0.at[(K + 1) * C : (K + 2) * C])
    ld_w1 = load(w1_hbm, w1)
    ld_rl = load(rl_hbm.at[:, 0:HEAD], rcat.at[0:C])
    ld_ru = load(ru_hbm.at[:, 0:HEAD], rcat.at[C : 2 * C])
    ld_w2 = load(w23_hbm.at[0 : K * C], w2.at[0 : K * C])
    ld_w2m = load(ru_hbm.at[:, HEAD + PRE : HEAD + PRE + WIDE], w2.at[K * C : (K + 1) * C])
    ld_w3 = load(w23_hbm.at[K * C : 2 * K * C], w3)

    bar = pltpu.get_barrier_semaphore()
    pl.semaphore_signal(bar, inc=1, device_id={"ch": sib}, device_id_type=MESH)
    for d in range(1, nz):
        pl.semaphore_signal(bar, inc=1, device_id=chip(lax.rem(z + d, nz), q), device_id_type=MESH)
    for d in range(1, nb):
        pl.semaphore_signal(bar, inc=1, device_id={"batch": lax.rem(b + d, nb)}, device_id_type=MESH)

    colbuf[...] = jnp.zeros_like(colbuf)
    rowbuf[...] = jnp.zeros_like(rowbuf)
    prm[...] = jnp.zeros_like(prm)
    prm[0, 0:11, 0:C] = lg_ref[...]
    prm[1, 0:11, 0:C] = lsh_ref[...]
    prm[2, 0:12, 0:C] = ug_ref[...]
    prm[3, 0:12, 0:C] = ush_ref[...]
    length = length_ref[0]
    lane_row = lax.broadcasted_iota(jnp.int32, (1, T), 1)
    valid = jnp.where(lane_row < length, 1.0, 0.0).astype(F32)
    valid_rb = jnp.broadcast_to(valid, (RB, T))

    ld_raw.wait()
    valid_b = valid.astype(BF16)

    def mask_rows(i, _):
        src[pl.ds(mult(c * E + i * RB), RB), :] = raw[pl.ds(mult(i * RB), RB), :] * jnp.broadcast_to(
            valid_b, (RB, T)
        )
        return 0

    lax.fori_loop(0, E // RB, mask_rows, 0, unroll=2)
    pl.semaphore_wait(bar, 1 + (nz - 1) + (nb - 1))

    def entry_rows(n):
        return src.at[pn.late[n][2] : pn.late[n][2] + pn.step]

    def entry_hop(n, device):
        v = entry_rows(n)
        return rcopy(v, v, pn.s_entry + n, pn.s_entry + n, device)

    def entry_sib(n):
        i = pn.s_entry + len(pn.late) + n
        return rcopy(entry_rows(n), entry_rows(n), i, i, {"ch": sib})

    order = [n for n in range(len(pn.late))]
    below = chip(jnp.maximum(z - 1, 0), q)
    above = chip(jnp.minimum(z + 1, nz - 1), q)

    for n in order:
        zc, qc, _ = pn.late[n]

        @pl.when((q == qc) & (z == zc))
        def _():
            if zc > 0:
                entry_hop(n, below).start()
            if zc < nz - 1:
                v = entry_rows(n)
                rcopy(v, v, pn.s_tail + n, pn.s_entry + n, above).start()
            entry_sib(n).start()

    for n in order:
        zc, qc, _ = pn.late[n]

        @pl.when((q == qc) & (z < zc))
        def _():
            entry_hop(n, below).wait_recv()

            @pl.when(z > 0)
            def _():
                entry_hop(n, below).start()

            entry_sib(n).start()

        if zc < nz - 1:

            @pl.when((q == qc) & (z > zc))
            def _():
                entry_hop(n, above).wait_recv()

                @pl.when(z < nz - 1)
                def _():
                    entry_hop(n, above).start()

                entry_sib(n).start()

        @pl.when(q != qc)
        def _():
            entry_sib(n).wait_recv()

    def entry_drain():
        for n in order:
            zc, qc, _ = pn.late[n]

            @pl.when(q == qc)
            def _():
                entry_sib(n).wait_send()

            @pl.when((q == qc) & (z <= zc) & (z > 0))
            def _():
                entry_hop(n, below).wait_send()

            if zc < nz - 1:

                @pl.when((q == qc) & (z == zc))
                def _():
                    v = entry_rows(n)
                    rcopy(v, v, pn.s_tail + n, pn.s_entry + n, above).wait_send()

                @pl.when((q == qc) & (z > zc) & (z < nz - 1))
                def _():
                    entry_hop(n, above).wait_send()

    def sized(cc, body):
        @pl.when(cc < pn.full)
        def _():
            body(E)

        if pn.part:

            @pl.when(cc == pn.full)
            def _():
                body(pn.part)

    class Gather:
        def __init__(self, base, buf, rows, cut=False):
            self.base, self.buf, self.rows, self.cut = base, buf, rows, cut

        def each(self, zz, qq, body):
            cc = zz * 2 + qq
            if self.cut:
                sized(cc, lambda n: body(self.buf.at[pl.ds(mult(cc * self.rows), n)]))
            else:
                body(self.buf.at[pl.ds(mult(cc * self.rows), self.rows)])

        def start(self):
            def go(v):
                for d in range(1, nz):
                    zz = lax.rem(z + d, nz)
                    rcopy(v, v, self.base + zz, self.base + z, chip(zz, q)).start()
                rcopy(v, v, self.base + nz + z, self.base + nz + z, {"ch": sib}).start()

            self.each(z, q, go)

        def step(self, d):
            zz = lax.rem(z + d, nz)

            def go(v):
                rcopy(v, v, self.base + zz, self.base + zz, {"ch": sib}).wait_recv()
                rcopy(v, v, self.base + nz + zz, self.base + nz + zz, {"ch": sib}).start()

            self.each(zz, q, go)

        def end(self):
            for d in range(nz):
                zz = lax.rem(z + d, nz)
                i = self.base + nz + zz
                self.each(zz, other, lambda v: rcopy(v, v, i, i, {"ch": sib}).wait_recv())

        def drain(self):
            def go(v):
                for d in range(1, nz):
                    zz = lax.rem(z + d, nz)
                    rcopy(v, v, self.base + zz, self.base + z, chip(zz, q)).wait_send()

            self.each(z, q, go)
            for d in range(nz):
                zz = lax.rem(z + d, nz)
                i = self.base + nz + zz
                self.each(zz, q, lambda v: rcopy(v, v, i, i, {"ch": sib}).wait_send())

    def sum_copies(p):
        rows = SUM_ROWS[p]
        for d in range(1, nb):
            bb = lax.rem(b + d, nb)
            v = sums.at[p, b, 0:rows]
            yield bb, rcopy(v, v, pn.s_sum[p] + bb, pn.s_sum[p] + b, {"batch": bb})

    def sum_start(p):
        rows = SUM_ROWS[p]
        sums[p, b, 0:rows, :] = colbuf[...].T[0:rows, :]
        for _, cp in sum_copies(p):
            cp.start()

    def sum_finish(p):
        rows = SUM_ROWS[p]
        for bb, _ in sum_copies(p):
            v = sums.at[p, bb, 0:rows]
            rcopy(v, v, pn.s_sum[p] + bb, pn.s_sum[p] + bb, {"batch": bb}).wait_recv()
        total = sums[p, 0, 0:rows, :]
        for bb in range(1, nb):
            total = total + sums[p, bb, 0:rows, :]
        return total

    def columns(p, parts):
        at = 0
        for part in parts:
            rowbuf[at : at + part.shape[0], :] = part
            at += part.shape[0]
        kcol[p] = rowbuf[...].T

    def norm_rows(first, second, count, gain, shift):
        average = first / count
        scaling = lax.rsqrt(second / count - average * average + EPS)
        scale = scaling * gain
        return average, scaling, scale, shift - average * scale

    def blocks(body):
        def step(i, carry):
            body(pl.ds(mult(i * RB), RB))
            return carry

        lax.fori_loop(0, C // RB, step, 0)

    def at_row(base, r):
        return pl.ds(mult(base + r.start), RB)

    def lane_sum(v):
        return jnp.sum(v, axis=1, keepdims=True)

    def conv(w, x, y_index, extra):
        rows = (K * C) // 5

        def part(g, carry):
            r = pl.ds(mult(g * rows), rows)
            big[r, :] = dot(w[r, :], x)
            return carry

        lax.fori_loop(0, 5, part, 0)
        if extra:
            big[K * C : (K + extra) * C, :] = dot(w[K * C : (K + extra) * C, :], x)

        def add(i, carry):
            total = None
            for k in range(K):
                v = shifted(big[pl.ds(mult(k * C + i * RB), RB), :], k - K // 2)
                total = v if total is None else total + v
            ys[y_index, pl.ds(mult(i * RB), RB), :] = total
            return carry

        lax.fori_loop(0, C // RB, add, 0)

    def conv_sums(y_index, col):
        def body(r):
            y = ys[y_index, r, :] * valid_rb
            colbuf[r, col : col + 1] = lane_sum(y)
            colbuf[r, col + 1 : col + 2] = lane_sum(y * y)

        blocks(body)

    def slices(j):
        if j == 0:
            return src, HEAD, pn.iw0, xs0
        return (None, x1, x2, x3)[j], 0, pn.iw, xs.at[j - 1]

    def slice_copies(j):
        x, base, iw, target = slices(j)
        rows = up16(iw)
        for d in range(1, nb):
            bb = lax.rem(b + d, nb)
            if rows == iw:
                source = x.at[pl.ds(mult(base + bb * iw), iw)]
            else:
                source = xst.at[j, bb, 0:rows]
            there = target.at[:, pl.ds(mult(b * T, LANES), T)]
            yield bb, rcopy(source, there, pn.s_xs[j] + bb, pn.s_xs[j] + b, {"batch": bb})

    def slice_start(j):
        x, base, iw, target = slices(j)
        rows = up16(iw)
        here = pl.ds(mult(b * T, LANES), T)
        if rows == iw:
            target[:, here] = x[pl.ds(mult(base + b * iw), iw), :]
        else:
            for bb in range(nb):
                xst[j, bb, 0:rows, :] = jnp.zeros((rows, T), BF16)
                xst[j, bb, 0:iw, :] = x[base + bb * iw : base + (bb + 1) * iw, :]
            target[:, here] = xst[j, b, 0:rows, :]
        for _, cp in slice_copies(j):
            cp.start()

    def slice_finish(j):
        target = slices(j)[3]
        for bb, _ in slice_copies(j):
            v = target.at[:, pl.ds(mult(bb * T, LANES), T)]
            rcopy(v, v, pn.s_xs[j] + bb, pn.s_xs[j] + bb, {"batch": bb}).wait_recv()

    def dy_copies(j):
        v = dyg.at[j, :, pl.ds(mult(b * T, LANES), T)]
        for d in range(1, nb):
            bb = lax.rem(b + d, nb)
            yield bb, rcopy(v, v, pn.s_dy[j] + bb, pn.s_dy[j] + b, {"batch": bb})

    def dy_start(j):
        for _, cp in dy_copies(j):
            cp.start()

    def dy_finish(j):
        for bb, _ in dy_copies(j):
            v = dyg.at[j, :, pl.ds(mult(bb * T, LANES), T)]
            rcopy(v, v, pn.s_dy[j] + bb, pn.s_dy[j] + bb, {"batch": bb}).wait_recv()

    out_copies = []

    def weight_grad(j, out, first):
        _, _, iw, target = slices(j)
        slice_finish(j)
        dy_finish(j)
        rows = pn.group * C
        for g in range(K // pn.group):

            def build(u, carry):
                here = pl.ds(mult(u * T, LANES), T)
                dy = dyg[j, :, here]
                for i in range(pn.group):
                    k = g * pn.group + i
                    dgrp[i * C : (i + 1) * C, here] = shifted(dy, K // 2 - k)
                return carry

            lax.fori_loop(0, nb, build, 0)
            slot = len(out_copies) % 2
            if len(out_copies) >= 2 and not (j == 0 and g > 1):
                out_copies[-2].wait()
            grad = dot_last(dgrp[...], target[...])
            stage = gst if j == 0 else gout.at[slot]
            if j == 0 and g > 0:
                out_copies[-1].wait()
            stage[...] = grad[:, 0:iw]
            source = stage
            cp = pltpu.make_async_copy(
                source, out.at[first + g * rows : first + (g + 1) * rows], osem.at[slot]
            )
            cp.start()
            out_copies.append(cp)

    half = WIDE // 2
    hz = nz // 2
    upper_half = z // hz

    def shift_all(j):
        dy = dyg[j, :, pl.ds(mult(b * T, LANES), T)]
        for k in range(K):
            dbuf[k * C : (k + 1) * C, :] = shifted(dy, K // 2 - k)

    def back_rows(w, extra, lanes, to):
        rows = (K * C) // 5
        if extra:
            r = slice(K * C, (K + extra) * C)
            big[to, :] = dot_first(w[r, lanes], dbuf[r, :])
        else:
            r = pl.ds(0, rows)
            big[to, :] = dot_first(w[r, lanes], dbuf[r, :])

        def part(g, carry):
            r = pl.ds(mult(g * rows), rows)
            big[to, :] += dot_first(w[r, lanes], dbuf[r, :])
            return carry

        lax.fori_loop(0 if extra else 1, 5, part, 0)

    class Scatter:
        def __init__(self, n):
            self.base, self.part, self.sibs, self.recv = pn.s_rs[n], dxpart, dxsib.at[n], dxrecv.at[n]

        def rows(self, zz, qq):
            return pl.ds(mult((zz * 2 + qq) * C), C)

        def to_sib(self, zz):
            return rcopy(
                self.part.at[self.rows(zz, other)],
                self.sibs.at[zz],
                self.base + zz,
                self.base + zz,
                {"ch": sib},
            )

        def to_chip(self, zz):
            return rcopy(
                self.part.at[self.rows(zz, q)],
                self.recv.at[z],
                self.base + nz + zz,
                self.base + nz + z,
                chip(zz, q),
            )

        def compute(self, w, extra):
            for far in (1, 0):
                m = upper_half + far - 2 * upper_half * far
                at = pl.ds(mult(m * half, LANES), half)
                back_rows(w, extra, at, at)
                for i in range(hz):
                    zz = m * hz + i
                    r = self.rows(zz, other)
                    self.part[r, :] = big[r, :].astype(BF16)
                    self.to_sib(zz).start()

        def fold(self, zz):
            self.to_sib(zz).wait_recv()
            return big[self.rows(zz, q), :] + self.sibs[zz].astype(F32)

        def send(self):
            for i in range(hz):
                zz = (1 - upper_half) * hz + i
                self.part[self.rows(zz, q), :] = self.fold(zz).astype(BF16)
                self.to_chip(zz).start()
            for i in range(1, hz):
                zz = upper_half * hz + lax.rem(z - upper_half * hz + i, hz)
                self.part[self.rows(zz, q), :] = self.fold(zz).astype(BF16)
                self.to_chip(zz).start()
            hold[0] = self.fold(z)

        def end(self):
            total = hold[0]
            for d in range(1, nz):
                zz = lax.rem(z + d, nz)
                v = self.recv.at[zz]
                rcopy(v, v, self.base + nz + zz, self.base + nz + zz, {"ch": sib}).wait_recv()
                total = total + self.recv[zz].astype(F32)
            hold[0] = total
            self.drain()

        def drain(self):
            for d in range(nz):
                self.to_sib(lax.rem(z + d, nz)).wait_send()
            for d in range(1, nz):
                self.to_chip(lax.rem(z + d, nz)).wait_send()

    rest = Gather(pn.s_rest, src, E, cut=True)
    rest.start()
    ld_w0.wait()
    ld_w0l.wait()
    ld_w0u.wait()
    conv(w0, src[HEAD : HEAD + PRE, :], 0, 2)
    resid[8] = big[K * C : (K + 2) * C, :]
    conv_sums(0, 0)
    colbuf[0:C, 2:3] = jnp.broadcast_to(length.astype(F32), (C, 1))
    sum_start(0)
    total = sum_finish(0)
    count = jnp.broadcast_to(total[2:3, 0:1], (1, LANES))
    av, rsd, sc, off = norm_rows(total[0:1], total[1:2], count, prm[0, 0:1], prm[1, 0:1])
    columns(0, [sc, off, av, rsd])

    def activate(p, y_index, out):
        def body(r):
            v = ys[y_index, r, :] * kcol[p, r, 0:1] + kcol[p, r, 1:2]
            out[at_row(c * C, r), :] = (v * squash(v) * valid_rb).astype(BF16)

        blocks(body)

    activate(0, 0, x1)
    gx1 = Gather(pn.s_x[0], x1, C)
    gx1.start()
    slice_start(0)
    for d in range(1, nz):
        gx1.step(d)
    gx1.end()
    ld_w1.wait()
    conv(w1, x1[...], 1, 0)
    for d in range(1, nz):
        rest.step(d)
    rest.end()
    ld_rl.wait()
    ld_ru.wait()
    for s in range(8):
        at, width = pn.pieces[s]
        resid[s] = dot(rcat[:, at : at + width], src[at : at + width, :])

    def first_sums(r):
        y = ys[1, r, :] * valid_rb
        colbuf[r, 0:1] = lane_sum(y)
        colbuf[r, 10:11] = lane_sum(y * y)
        for s in range(9):
            v = resid[s, r, :]
            colbuf[r, 1 + s : 2 + s] = lane_sum(v)
            colbuf[r, 11 + s : 12 + s] = lane_sum(v * v)
            v = resid[s, at_row(C, r), :]
            colbuf[r, 20 + s : 21 + s] = lane_sum(v)
            colbuf[r, 29 + s : 30 + s] = lane_sum(v * v)

    blocks(first_sums)
    sum_start(1)
    total = sum_finish(1)
    lo = norm_rows(total[0:10], total[10:20], count, prm[0, 1:11], prm[1, 1:11])
    lo_scale_rows, lo_rsd_rows = lo[2], lo[1]
    off_sum = jnp.sum(lo[3], axis=0, keepdims=True)
    columns(1, [lo[2], lo[0], lo[1], off_sum])
    up_av, up_rsd, up_sc, up_off = norm_rows(total[20:29], total[29:38], count, prm[2, 2:11], prm[3, 2:11])
    up_off_sum = jnp.sum(up_off, axis=0, keepdims=True)

    def lower_value(r):
        v = ys[1, r, :] * kcol[1, r, 0:1] + kcol[1, r, 30:31]
        for s in range(9):
            v = v + resid[s, r, :] * kcol[1, r, 1 + s : 2 + s]
        return v

    def lower_out(r):
        v = lower_value(r)
        hold[1, r, :] = v
        x2[at_row(c * C, r), :] = (v * squash(v) * valid_rb).astype(BF16)

    blocks(lower_out)
    gx2 = Gather(pn.s_x[1], x2, C)
    gx2.start()
    slice_start(1)
    for d in range(1, nz):
        gx2.step(d)
    gx2.end()
    ld_w2.wait()
    ld_w2m.wait()
    conv(w2, x2[...], 2, 1)
    rmid[...] = big[K * C : (K + 1) * C, :]
    conv_sums(2, 0)

    def mid_sums(r):
        v = rmid[r, :]
        colbuf[r, 2:3] = lane_sum(v)
        colbuf[r, 3:4] = lane_sum(v * v)

    blocks(mid_sums)
    sum_start(2)
    total = sum_finish(2)
    u2 = norm_rows(total[0:1], total[1:2], count, prm[2, 0:1], prm[3, 0:1])
    mid = norm_rows(total[2:3], total[3:4], count, prm[2, 11:12], prm[3, 11:12])
    columns(2, [u2[2], u2[3], u2[0], u2[1]])
    activate(2, 2, x3)
    gx3 = Gather(pn.s_x[2], x3, C)
    gx3.start()
    slice_start(2)
    for d in range(1, nz):
        gx3.step(d)
    gx3.end()
    ld_w3.wait()
    conv(w3, x3[...], 3, 0)
    conv_sums(3, 0)
    sum_start(3)
    total = sum_finish(3)
    u3 = norm_rows(total[0:1], total[1:2], count, prm[2, 1:2], prm[3, 1:2])
    up_scale_rows = [u3[2], up_sc, mid[2]]
    columns(
        3,
        [
            u3[2], up_sc, mid[2],
            u3[0], up_av, mid[0],
            u3[1], up_rsd, mid[1],
            u3[3] + up_off_sum + mid[3],
        ],
    )

    def value_back(v, gradient):
        s = squash(v)
        return gradient * valid_rb * s * (1.0 + v * (1.0 - s))

    def upper_out(r):
        v = ys[3, r, :] * kcol[3, r, 0:1] + kcol[3, r, 33:34]
        for s in range(9):
            v = v + resid[s, at_row(C, r), :] * kcol[3, r, 1 + s : 2 + s]
        v = v + rmid[r, :] * kcol[3, r, 10:11]
        final_ref[r, :] = (v * squash(v) * valid_rb).astype(BF16)
        dv = value_back(v, cot_ref[r, :].astype(F32))
        hold[2, r, :] = dv
        colbuf[r, 0:1] = lane_sum(dv)
        colbuf[r, 1:2] = lane_sum(dv * (ys[3, r, :] - kcol[3, r, 11:12])) * kcol[3, r, 22:23]
        for s in range(9):
            centred = resid[s, at_row(C, r), :] - kcol[3, r, 12 + s : 13 + s]
            colbuf[r, 2 + s : 3 + s] = lane_sum(dv * centred) * kcol[3, r, 23 + s : 24 + s]
        centred = rmid[r, :] - kcol[3, r, 21:22]
        colbuf[r, 11:12] = lane_sum(dv * centred) * kcol[3, r, 32:33]

    blocks(upper_out)
    sum_start(4)
    total = sum_finish(4)
    slice_start(3)
    upper_q = total[0:1]
    upper_g = total[1:12]
    usg_ref[1:12, :] = jnp.broadcast_to(upper_q[:, 0:C], (11, C))
    ugg_ref[1:12, :] = upper_g[:, 0:C]
    sc_rows = jnp.concatenate(up_scale_rows, axis=0)
    rsd_rows = jnp.concatenate([u3[1], up_rsd, mid[1]], axis=0)
    columns(4, [sc_rows * upper_q / count, sc_rows * rsd_rows * upper_g / count])

    def grad_rows(gradient, values, sc_col, av_col, a_col, b_col):
        return ((sc_col * gradient - (a_col + b_col * (values - av_col))) * valid_rb).astype(BF16)

    own_lanes = pl.ds(mult(b * T, LANES), T)

    def upper_dy(r):
        dyg[3, r, own_lanes] = grad_rows(
            hold[2, r, :], ys[3, r, :], kcol[3, r, 0:1], kcol[3, r, 11:12], kcol[4, r, 0:1], kcol[4, r, 11:12]
        )

    blocks(upper_dy)
    shift_all(3)
    sc0 = Scatter(0)
    sc0.compute(w3, 0)
    sc0.send()
    dy_start(3)

    def upper_dr(r):
        dv = hold[2, r, :]
        for s in range(9):
            drcat[s, at_row(C, r), :] = grad_rows(
                dv,
                resid[s, at_row(C, r), :],
                kcol[3, r, 1 + s : 2 + s],
                kcol[3, r, 12 + s : 13 + s],
                kcol[4, r, 1 + s : 2 + s],
                kcol[4, r, 12 + s : 13 + s],
            )
        dbuf[at_row(K * C, r), :] = grad_rows(
            dv, rmid[r, :], kcol[3, r, 10:11], kcol[3, r, 21:22], kcol[4, r, 10:11], kcol[4, r, 21:22]
        )

    blocks(upper_dr)

    def dense_stage(n, first_col, value):
        share = (pn.all + (WIDE if n else 0)) // nb
        end = first_col + value.shape[1]
        for bb in range(nb):
            lo_c, hi_c = max(first_col, bb * share), min(end, (bb + 1) * share)
            if lo_c < hi_c:
                drs[n, bb, :, lo_c - bb * share : hi_c - bb * share] = value[
                    :, lo_c - first_col : hi_c - first_col
                ].astype(BF16)

    def dense_copies(n):
        for d in range(1, nb):
            bb = lax.rem(b + d, nb)
            yield bb, rcopy(drs.at[n, bb], drr.at[n, b], pn.s_dr[n] + bb, pn.s_dr[n] + b, {"batch": bb})

    def dense_start(n):
        for _, cp in dense_copies(n):
            cp.start()

    def dense_finish(n, out):
        share = (pn.all + (WIDE if n else 0)) // nb
        total = drs[n, b, :, 0:share].astype(F32)
        for bb, _ in dense_copies(n):
            v = drr.at[n, bb]
            rcopy(v, v, pn.s_dr[n] + bb, pn.s_dr[n] + bb, {"batch": bb}).wait_recv()
            total = total + drr[n, bb, :, 0:share].astype(F32)
        out[...] = total

    for s in range(9):
        at, width = pn.pieces[s]
        dense_stage(1, at, dot_last(drcat[s, C : 2 * C, :], src[at : at + width, :]))
    dense_stage(1, HEAD + PRE, dot_last(dbuf[K * C : (K + 1) * C, :], x2[...]))
    sc0.end()

    def inner_back(p, y_index):
        def body(r):
            y = ys[y_index, r, :]
            dz = value_back(y * kcol[p, r, 0:1] + kcol[p, r, 1:2], hold[0, r, :])
            hold[3, r, :] = dz
            colbuf[r, 0:1] = lane_sum(dz)
            colbuf[r, 1:2] = lane_sum(dz * (y - kcol[p, r, 2:3])) * kcol[p, r, 3:4]

        blocks(body)

    def inner_dy(p, kept, y_index):
        def body(r):
            dyg[y_index, r, own_lanes] = grad_rows(
                hold[3, r, :], ys[y_index, r, :], kcol[kept, r, 0:1], kcol[kept, r, 2:3], kcol[p, r, 0:1], kcol[p, r, 1:2]
            )

        blocks(body)

    inner_back(2, 2)
    sum_start(5)
    total = sum_finish(5)
    dense_start(1)
    usg_ref[0:1, :] = total[0:1, 0:C]
    ugg_ref[0:1, :] = total[1:2, 0:C]
    columns(5, [u2[2] * total[0:1] / count, u2[2] * u2[1] * total[1:2] / count])
    inner_dy(5, 2, 2)
    shift_all(2)
    sc1 = Scatter(1)
    sc1.compute(w2, 1)
    sc1.send()
    dy_start(2)
    weight_grad(3, g23_hbm, K * C)
    sc1.end()

    def lower_back(r):
        v = hold[1, r, :]
        dv = value_back(v, hold[0, r, :])
        hold[2, r, :] = dv
        colbuf[r, 0:1] = lane_sum(dv)
        colbuf[r, 1:2] = lane_sum(dv * (ys[1, r, :] - kcol[1, r, 10:11])) * kcol[1, r, 20:21]
        for s in range(9):
            centred = resid[s, r, :] - kcol[1, r, 11 + s : 12 + s]
            colbuf[r, 2 + s : 3 + s] = lane_sum(dv * centred) * kcol[1, r, 21 + s : 22 + s]

    blocks(lower_back)
    sum_start(6)
    total = sum_finish(6)
    lower_q = total[0:1]
    lower_g = total[1:11]
    lsg_ref[1:11, :] = jnp.broadcast_to(lower_q[:, 0:C], (10, C))
    lgg_ref[1:11, :] = lower_g[:, 0:C]
    columns(6, [lo_scale_rows * lower_q / count, lo_scale_rows * lo_rsd_rows * lower_g / count])

    def lower_dy(r):
        dyg[1, r, own_lanes] = grad_rows(
            hold[2, r, :], ys[1, r, :], kcol[1, r, 0:1], kcol[1, r, 10:11], kcol[6, r, 0:1], kcol[6, r, 10:11]
        )

    blocks(lower_dy)
    shift_all(1)
    sc2 = Scatter(2)
    sc2.compute(w1, 0)
    sc2.send()
    dy_start(1)

    def lower_dr(r):
        dv = hold[2, r, :]
        for s in range(9):
            drcat[s, r, :] = grad_rows(
                dv,
                resid[s, r, :],
                kcol[1, r, 1 + s : 2 + s],
                kcol[1, r, 11 + s : 12 + s],
                kcol[6, r, 1 + s : 2 + s],
                kcol[6, r, 11 + s : 12 + s],
            )

    blocks(lower_dr)

    for s in range(8):
        at, width = pn.pieces[s]
        dpart[at : at + width, :] = dot_first(rcat[:, at : at + width], drcat[s]).astype(BF16)

    def dp_rows(zz, qq, n):
        return pl.ds(mult((zz * 2 + qq) * E), n)

    def dp_sib(zz, n):
        return rcopy(
            dpart.at[dp_rows(zz, other, n)], dpsib.at[zz, 0:n], pn.s_dp + zz, pn.s_dp + zz, {"ch": sib}
        )

    def dp_sib_in(zz, n):
        v = dpsib.at[zz, 0:n]
        return rcopy(v, v, pn.s_dp + zz, pn.s_dp + zz, {"ch": sib})

    def dp_chip(zz, n):
        return rcopy(
            dpart.at[dp_rows(zz, q, n)],
            dprecv.at[z, 0:n],
            pn.s_dp + nz + zz,
            pn.s_dp + nz + z,
            chip(zz, q),
        )

    def dp_in(zz, n):
        v = dprecv.at[zz, 0:n]
        return rcopy(v, v, pn.s_dp + nz + zz, pn.s_dp + nz + zz, {"ch": sib})

    for d in range(nz):
        zz = lax.rem(z + d, nz)
        sized(zz * 2 + other, lambda n: dp_sib(zz, n).start())

    def dp_fold(zz, n):
        def body(i, carry):
            here = pl.ds(mult(i * RB), RB)
            there = pl.ds(mult((zz * 2 + q) * E + i * RB), RB)
            dpart[there, :] = (dpart[there, :].astype(F32) + dpsib[zz, here, :].astype(F32)).astype(BF16)
            return carry

        lax.fori_loop(0, n // RB, body, 0)

    for d in range(1, nz):
        zz = lax.rem(z + d, nz)

        def go(n):
            dp_sib_in(zz, n).wait_recv()
            dp_fold(zz, n)
            dp_chip(zz, n).start()

        sized(zz * 2 + q, go)

    def go_own(n):
        dp_sib_in(z, n).wait_recv()
        dp_fold(z, n)

    sized(c, go_own)
    weight_grad(2, g23_hbm, 0)
    sc2.end()

    inner_back(0, 0)
    sum_start(7)
    total = sum_finish(7)
    lsg_ref[0:1, :] = total[0:1, 0:C]
    lgg_ref[0:1, :] = total[1:2, 0:C]
    l0_scale = kcol[0].T
    columns(7, [l0_scale[0:1] * total[0:1] / count, l0_scale[0:1] * l0_scale[3:4] * total[1:2] / count])
    inner_dy(7, 0, 0)
    shift_all(0)
    dbuf[K * C : (K + 2) * C, :] = drcat[8]
    cut = (PRE // 2 + LANES - 1) // LANES * LANES
    back_rows(w0, 2, slice(0, cut), slice(0, cut))
    back_rows(w0, 2, slice(cut, PRE), slice(cut, PRE))
    dy_start(0)

    count_late = len(pn.late)

    def tail_rows(n):
        return dpart.at[pn.late[n][2] : pn.late[n][2] + pn.step]

    def tail_sib(n):
        return rcopy(tail_rows(n), tailsib.at[n], pn.s_tail + n, pn.s_tail + n, {"ch": sib})

    def tail_hop(n, way, device):
        i = pn.s_tail + (1 + way) * count_late + n
        return rcopy(tail_rows(n), tailrecv.at[way, n], i, i, device)

    for n in range(count_late):
        zc, qc, row = pn.late[n]

        @pl.when(q != qc)
        def _():
            dpart[row : row + pn.step, :] = big[row - HEAD : row - HEAD + pn.step, :].astype(BF16)
            tail_sib(n).start()

    for n in range(count_late):
        zc, qc, row = pn.late[n]
        here = slice(row, row + pn.step)
        there = slice(row - HEAD, row - HEAD + pn.step)

        @pl.when(q == qc)
        def _():
            tail_sib(n).wait_recv()
            big[there, :] += tailsib[n].astype(F32)
            if zc > 0:

                @pl.when((z > 0) & (z <= zc))
                def _():
                    tail_hop(n, 0, above).wait_recv()
                    big[there, :] += tailrecv[0, n].astype(F32)

            if zc < nz - 1:

                @pl.when((z < nz - 1) & (z >= zc))
                def _():
                    tail_hop(n, 1, below).wait_recv()
                    big[there, :] += tailrecv[1, n].astype(F32)

            @pl.when(z < zc)
            def _():
                dpart[here, :] = big[there, :].astype(BF16)
                tail_hop(n, 0, above).start()

            if zc < nz - 1:

                @pl.when(z > zc)
                def _():
                    dpart[here, :] = big[there, :].astype(BF16)
                    tail_hop(n, 1, below).start()

            @pl.when(z == zc)
            def _():
                big[WIDE + row % E : WIDE + row % E + pn.step, :] = big[there, :] * valid

    for s in range(9):
        at, width = pn.pieces[s]
        dense_stage(0, at, dot_last(drcat[s, 0:C, :], src[at : at + width, :]))
    dense_start(0)
    weight_grad(1, g1_hbm, 0)
    weight_grad(0, g0_hbm, 0)
    dense_finish(1, rug_ref)

    def own_grad(n):
        for d in range(1, nz):
            dp_in(lax.rem(z + d, nz), n).wait_recv()

        def body(i, carry):
            here = pl.ds(mult(i * RB), RB)
            total = dpart[pl.ds(mult(c * E + i * RB), RB), :].astype(F32)
            for d in range(1, nz):
                total = total + dprecv[lax.rem(z + d, nz), here, :].astype(F32)
            big[pl.ds(mult(WIDE + i * RB), RB), :] = total * valid_rb
            return carry

        lax.fori_loop(0, n // RB, body, 0)

    sized(c, own_grad)
    egrad_copy = pltpu.make_async_copy(big.at[WIDE : WIDE + E], egrad_hbm, osem.at[2])
    egrad_copy.start()
    dense_finish(0, rlg_ref)

    out_copies[-1].wait()
    egrad_copy.wait()
    entry_drain()
    for g in (rest, gx1, gx2, gx3):
        g.drain()
    for p in range(8):
        for _, cp in sum_copies(p):
            cp.wait_send()
    for j in range(4):
        for _, cp in slice_copies(j):
            cp.wait_send()
        for _, cp in dy_copies(j):
            cp.wait_send()
    for n in range(2):
        for _, cp in dense_copies(n):
            cp.wait_send()
    for d in range(nz):
        zz = lax.rem(z + d, nz)
        sized(zz * 2 + other, lambda n: dp_sib(zz, n).wait_send())
    for d in range(1, nz):
        zz = lax.rem(z + d, nz)
        sized(zz * 2 + q, lambda n: dp_chip(zz, n).wait_send())
    for n in range(count_late):
        zc, qc, _ = pn.late[n]

        @pl.when(q != qc)
        def _():
            tail_sib(n).wait_send()

        @pl.when((q == qc) & (z < zc))
        def _():
            tail_hop(n, 0, above).wait_send()

        if zc < nz - 1:

            @pl.when((q == qc) & (z > zc))
            def _():
                tail_hop(n, 1, below).wait_send()


def per_device(
    nb,
    nc,
    earlier,
    lengths,
    lower_entry,
    lower_convs,
    upper_convs,
    lower_dense,
    upper_dense,
    lower_gain,
    lower_shift,
    upper_gain,
    upper_shift,
    cotangent,
):
    _, own, frames = earlier.shape
    taps, cw, pre = lower_entry.shape
    pn = Plan(nb, nc, own, frames, taps, cw, pre)
    T, K, C, E, WIDE, nz = frames, taps, cw, own, pn.wide, pn.nz
    late = len(pn.late)
    share = ((pn.all + WIDE) // nb + LANES - 1) // LANES * LANES
    w0p, wp = up16(pn.iw0), up16(pn.iw)
    staged = 4 if (w0p != pn.iw0 or wp != pn.iw) else 1
    vmem, any_ = pl.BlockSpec(memory_space=pltpu.VMEM), pl.BlockSpec(memory_space=pl.ANY)
    smem = pl.BlockSpec(memory_space=pltpu.SMEM)
    V = pltpu.VMEM
    scratch = [
        V(((K + 2) * C, pre), BF16),
        V((K * C, WIDE), BF16),
        V(((K + 1) * C, WIDE), BF16),
        V((K * C, WIDE), BF16),
        V((2 * C, pn.head), BF16),
        V((pn.all, T), BF16),
        V((WIDE, T), BF16),
        V((WIDE, T), BF16),
        V((WIDE, T), BF16),
        V(((K + 2) * C, T), F32),
        V((9, 2 * C, T), F32),
        V((C, T), F32),
        V((4, C, T), F32),
        V(((K + 2) * C, T), BF16),
        V((pn.group * C, nb * T), BF16),
        V((9, 2 * C, T), BF16),
        V((pn.all, T), BF16),
        V((nz, E, T), BF16),
        V((nz, E, T), BF16),
        V((WIDE, T), BF16),
        V((3, nz, C, T), BF16),
        V((3, nz, C, T), BF16),
        V((late, pn.step, T), BF16),
        V((1 + (pn.late[0][0] < nz - 1), late, pn.step, T), BF16),
        V((4, C, nb * T), BF16),
        V((w0p, nb * T), BF16),
        V((3, wp, nb * T), BF16),
        V((4, nb, max(w0p, wp), T) if staged == 4 else (1, 1, 16, T), BF16),
        V((2, nb, C, share), BF16),
        V((2, nb, C, share), BF16),
        V((8, nb, 40, LANES), F32),
        V((LANES, LANES), F32),
        V((LANES, LANES), F32),
        V((8, LANES, LANES), F32),
        V((4, 16, LANES), F32),
        V((4, C, T), F32),
        V((2, pn.group * C, pn.iw), F32),
        V((pn.group * C, pn.iw0), F32),
        pltpu.SemaphoreType.DMA((10,)),
        pltpu.SemaphoreType.DMA((3,)),
        pltpu.SemaphoreType.DMA((pn.sems,)),
        pltpu.SemaphoreType.DMA((pn.sems,)),
    ]
    shape = jax.ShapeDtypeStruct
    outs = pl.pallas_call(
        functools.partial(kernel, pn),
        out_shape=(
            shape((C, T), BF16),
            shape((E, T), F32),
            shape((K * C, pn.iw0), F32),
            shape((K * C, pn.iw), F32),
            shape((2 * K * C, pn.iw), F32),
            shape((C, pn.all // nb), F32),
            shape((C, (pn.all + WIDE) // nb), F32),
            shape((11, C), F32),
            shape((11, C), F32),
            shape((12, C), F32),
            shape((12, C), F32),
        ),
        in_specs=[smem] + [any_] * 6 + [vmem] * 5,
        out_specs=(vmem, any_, any_, any_, any_, vmem, vmem, vmem, vmem, vmem, vmem),
        scratch_shapes=scratch,
        compiler_params=pltpu.CompilerParams(
            collective_id=0, has_side_effects=True, vmem_limit_bytes=64000 * 1024
        ),
    )(
        lengths,
        earlier.reshape(own, frames),
        lower_entry.reshape(K * C, pre),
        lower_convs.reshape(K * C, WIDE),
        upper_convs.reshape(2 * K * C, WIDE),
        lower_dense,
        upper_dense,
        lower_gain,
        lower_shift,
        upper_gain,
        upper_shift,
        cotangent.reshape(C, T),
    )
    final, egrad, g0, g1, g23, rlg, rug, lgg, lsg, ugg, usg = outs
    return (
        final.reshape(1, C, T),
        egrad.reshape(1, E, T),
        g0.reshape(K, C, pn.iw0),
        g1.reshape(1, K, C, pn.iw),
        g23.reshape(2, K, C, pn.iw),
        rlg,
        rug,
        lgg,
        lsg,
        ugg,
        usg,
    )


def solution(mesh):
    placed = (
        P("batch", "ch", None),
        P("batch"),
        P(None, "ch", None),
        P(None, None, "ch", None),
        P(None, None, "ch", None),
        P("ch", None),
        P("ch", None),
        P(None, "ch"),
        P(None, "ch"),
        P(None, "ch"),
        P(None, "ch"),
        P("batch", "ch", None),
    )
    return jax.shard_map(
        functools.partial(per_device, mesh.shape["batch"], mesh.shape["ch"]),
        mesh=mesh,
        in_specs=placed,
        out_specs=(
            P("batch", "ch", None),
            P("batch", "ch", None),
            P(None, "ch", "batch"),
            P(None, None, "ch", "batch"),
            P(None, None, "ch", "batch"),
            P("ch", "batch"),
            P("ch", "batch"),
            P(None, "ch"),
            P(None, "ch"),
            P(None, "ch"),
            P(None, "ch"),
        ),
        check_vma=False,
    )
```

time: 919 us -> 291 us (0.32); the launches traced: 902 us -> 291 us
  Pallas kernels: 0 us -> 276 us
  local copies, waits for them, and re-layouts: 279 us -> 13.8 us
  matrix products: 218 us -> 0 us
  waiting for transfers between devices: 182 us -> 0 us
  blocking collectives: 128 us -> 0 us
  other arithmetic: 77.5 us -> 0 us
  between operations: 16.1 us -> 1.36 us
    pallas_call x0 -> x1, Pallas kernels: none -> 276 us  [per_device(): pl.pallas_call(functools.partial(kernel, pn), out_shape=(shape((C, T), BF...]
    conv_general_dilated x12 -> x0, matrix products: 132 us -> none  [the longest x4 84.6 us: conv_weight_grad(): lax.conv_general_dilated(padded, gradient, (1,), [(0, 0)], dimension_numb...]
    dot_general x57 -> x0, matrix products: 85.4 us -> none  [the longest x19 31.6 us: block_backward(): jnp.einsum('oi,uot->uit', dense_weight[:, offset:offset + channels], grad...]
    unnamed x17 -> x0, waiting for transfers between devices: 79 us -> none
    unnamed x162 -> x31, local copies, waits for them, and re-layouts: 92.6 us -> 13.8 us
    psum x8 -> x0, blocking collectives: 72.1 us -> none  [the longest x4 36.8 us: block_forward(): lax.psum((first_sum, second, dense_first, dense_second, local_count), 'ba...]
    conv_general_dilated x36 -> x0, local copies, waits for them, and re-layouts: 64.3 us -> none  [the longest x20 44.4 us: conv_apply(): lax.conv_general_dilated(inputs, weight, (1,), [(before, kernel_taps - 1...]
    reduce_scatter x4 -> x0, waiting for transfers between devices: 61.9 us -> none  [weight_gradient(): lax.psum_scatter(conv_weight_grad(inputs, grad_conv, kernel_taps).astype(...]
  transfers between devices with their start and end apart: 11 -> 0, of which waited for: 7 -> 0; matrix products, arithmetic and copies ran while one was open for 32% -> 0% of each run, Pallas kernels for 0% -> 0%
where the time goes in v1:
time: 291 us
  Pallas kernels  276 us (95%)
  local copies, waits for them, and re-layouts  13.8 us (5%)
    pallas_call x1, Pallas kernels, per_device(): pl.pallas_call(functools.partial(kernel, pn), out_shape=(shape((C, T), BF...  276 us
    unnamed x31, local copies, waits for them, and re-layouts  13.8 us

profile of v1, /device:TPU:25, one launch (start us, length us, event | category | flops | bytes accessed | tf_op | source)
XLA Modules:
  0.0 290.7 jit_solution(16727747139173253230)
XLA Ops:
  1.3 275.5 %shard_map.203 = (bf16[96,512]{1,0:T(8,128)(2,1)}, f32[480,512]{1,0:T(8,128)}, f32[2400,160]{1,0:T(8,128)}, f32[2400,192]{1,0:T(8,128)}, f32[4800,192]{1,0:T(8,1...) custom-call(s32[1]{0:T(128)S(6)} %copy.34.length_ref, ...), custom_call_target="tpu_custom_call" | custom-call | tf_op jit(solution)/shard_map/pallas_call | solution.py:1207
  276.8 0.0 copy-start.5
  276.9 0.0 copy-start.2
  276.9 0.0 copy-start.1
  276.9 3.3 %copy.23 = f32[25,96,160]{1,2,0:T(8,128)} copy(f32[25,96,160]{2,1,0:T(8,128)} %bitcast.15) | data formatting | bytes 3072000
  280.2 0.0 copy-done.5
  280.2 0.6 copy.35
  280.9 0.0 copy-done.2
  280.9 0.0 copy-start
  280.9 0.9 copy.36
  281.8 0.0 copy-done.1
  281.8 1.4 copy.37
  283.3 1.2 copy-done
  284.5 0.0 copy-start.4
  284.5 0.0 copy-start.3
  284.5 0.0 copy-start.9
  284.5 0.0 copy-start.8
  284.5 0.0 copy-start.7
  284.5 0.0 copy-start.6
  284.5 2.3 copy.38
  286.8 0.0 copy-done.4
  286.8 0.7 copy.39
  287.5 0.0 copy-done.3
  287.5 0.8 copy.40
  288.3 0.0 copy-done.9
  288.3 0.6 copy.41
  288.9 0.0 copy-done.8
  288.9 0.6 copy.42
  289.5 0.0 copy-done.7
  289.5 0.6 copy.43
  290.1 0.0 copy-done.6
  290.1 0.6 copy.44
Async XLA Ops:
  276.8 3.4 %copy-start.5 = (bf16[96,512]{1,0:T(8,128)(2,1)S(1)}, bf16[96,512]{1,0:T(8,128)(2,1)}, u32[]{:S(2)}) copy-start(bf16[96,512]{1,0:T(8,128)(2,1)} %get-tuple-element.22) | copy-start | bytes 294916
  276.9 4.0 %copy-start.2 = (f32[480,512]{1,0:T(8,128)S(1)}, f32[480,512]{1,0:T(8,128)}, u32[]{:S(2)}) copy-start(f32[480,512]{1,0:T(8,128)} %get-tuple-element.23) | copy-start | bytes 2949124
  276.9 5.0 %copy-start.1 = (f32[2400,192]{1,0:T(8,128)S(1)}, f32[2400,192]{1,0:T(8,128)}, u32[]{:S(2)}) copy-start(f32[2400,192]{1,0:T(8,128)} %get-tuple-element.25) | copy-start | bytes 5529604
  280.9 3.6 %copy-start = (f32[4800,192]{1,0:T(8,128)S(1)}, f32[4800,192]{1,0:T(8,128)}, u32[]{:S(2)}) copy-start(f32[4800,192]{1,0:T(8,128)} %get-tuple-element.26) | copy-start | bytes 11059204
  284.5 2.3 copy-start.4
  284.5 3.0 %copy-start.3 = (f32[96,1152]{1,0:T(8,128)S(1)}, f32[96,1152]{1,0:T(8,128)}, u32[]{:S(2)}) copy-start(f32[96,1152]{1,0:T(8,128)} %get-tuple-element.61) | copy-start | bytes 1327108
  284.5 3.8 %copy-start.9 = (f32[11,96]{1,0:T(8,128)S(1)}, f32[11,96]{1,0:T(8,128)}, u32[]{:S(2)}) copy-start(f32[11,96]{1,0:T(8,128)} %get-tuple-element.62) | copy-start | bytes 12676
  284.5 4.4 %copy-start.8 = (f32[11,96]{1,0:T(8,128)S(1)}, f32[11,96]{1,0:T(8,128)}, u32[]{:S(2)}) copy-start(f32[11,96]{1,0:T(8,128)} %get-tuple-element.63) | copy-start | bytes 12676
  284.5 5.0 %copy-start.7 = (f32[12,96]{1,0:T(8,128)S(1)}, f32[12,96]{1,0:T(8,128)}, u32[]{:S(2)}) copy-start(f32[12,96]{1,0:T(8,128)} %get-tuple-element.64) | copy-start | bytes 13828
  284.5 5.6 %copy-start.6 = (f32[12,96]{1,0:T(8,128)S(1)}, f32[12,96]{1,0:T(8,128)}, u32[]{:S(2)}) copy-start(f32[12,96]{1,0:T(8,128)} %get-tuple-element.65) | copy-start | bytes 13828
